TPU v7x, 32 devices: a whole 2x2x4 slice. The times are simulated.
32 devices in a mesh: layer: 4 (over y, x), row: 2 (over core), col: 4 (over z).
Axes of the slice: x: 2, y: 2, z: 4, core: 2. Of those that a mesh axis runs over, the one named last changes fastest.
Arguments:
- density: bfloat16 [2048, 2048], P('row', 'col'), may hold values from -0.25 to 0.25
- hamiltonian: bfloat16 [2048, 2048], P('row', 'col'), may hold values from -6 to 6
- density_mask: int32 [32, 32], P('row', 'col'), may hold values from 0 to 1, as said below
- hamilton_mask: int32 [32, 32], P('row', 'col'), may hold values from 0 to 1, as said below
- filter_mask: int32 [32, 32], P('row', 'col'), may hold values from 0 to 1, as said below
Outputs:
- weighted: bfloat16 [2048, 2048], P('row', 'col')
Inputs may be any that keep to these rules, and one draw needn't show every extreme that they name: `density_mask`: each entry is 0 or 1; diagonal blocks are 1. `hamilton_mask`: each entry is 0 or 1; diagonal blocks are 1. `filter_mask`: each entry is 0 or 1; diagonal blocks are 1.
All inputs are finite; a program needn't handle non-finite values.
Results may differ from a plain program's by a relative error of at most 0.005.
Values may be sent and summed in bfloat16 or wider, within the bound.
A program may use at most 64 MiB of HBM per device.

v0:
```python
import jax
import jax.numpy as jnp
from jax import lax
from jax.sharding import PartitionSpec as P

BS = 64


def expand_mask(mask_blocks):
    return jnp.repeat(jnp.repeat(mask_blocks, BS, axis=0), BS, axis=1).astype(jnp.bfloat16)


def inner_rows(matrix, groups, width, layer_pos):
    pieces = []
    stride = matrix.shape[0] // groups
    for group in range(groups):
        offset = group * stride + layer_pos * width
        pieces.append(lax.dynamic_slice_in_dim(matrix, offset, width, 0))
    return jnp.concatenate(pieces, axis=0)


def local(density, hamiltonian, density_mask, hamilton_mask, filter_mask):
    layers = lax.axis_size("layer")
    layer_pos = lax.axis_index("layer")
    groups = lax.axis_size("col") // lax.axis_size("row")
    tile_rows, tile_cols = density.shape
    width = tile_cols // layers
    masked_p = density * expand_mask(density_mask)
    masked_h = hamiltonian * expand_mask(hamilton_mask)
    h_inner = lax.all_gather(
        inner_rows(masked_h, groups, width, layer_pos), "row", axis=0, tiled=True
    )
    p_share = lax.dynamic_slice_in_dim(masked_p, layer_pos * width, width, 1)
    rows = h_inner
    partial_q = jnp.dot(
        lax.all_gather(p_share, "col", axis=1, tiled=True), rows, preferred_element_type=jnp.float32
    )
    summed_q = lax.psum_scatter(partial_q, "layer", scatter_dimension=1, tiled=True)
    filter_share = lax.dynamic_slice_in_dim(filter_mask, layer_pos * (width // BS), width // BS, 1)
    product = summed_q.astype(jnp.bfloat16) * expand_mask(filter_share)
    p_inner = lax.all_gather(
        inner_rows(masked_p, groups, width, layer_pos), "row", axis=0, tiled=True
    )
    rows = p_inner
    partial_w = jnp.dot(
        lax.all_gather(product, "col", axis=1, tiled=True), rows, preferred_element_type=jnp.float32
    )
    weighted = lax.psum(partial_w, "layer").astype(jnp.bfloat16)
    return weighted


def solution(mesh):
    placed = (P("row", "col"), P("row", "col"), P("row", "col"), P("row", "col"), P("row", "col"))
    return jax.shard_map(
        local, mesh=mesh, in_specs=placed, out_specs=P("row", "col"), check_vma=False
    )
```

profile of v0, /device:TPU:0, one launch (start us, length us, event | category | flops | bytes accessed | tf_op | source)
XLA Modules:
  0.0 191.7 jit_solution(7376734789413671161)
XLA Ops:
  6.5 1.6 copy.9
  8.1 0.1 broadcast_in_dim.18
  8.2 0.1 convert_element_type.40
  8.3 0.1 bitcast_multiply_fusion.1
  8.4 0.7 constant_dynamic-slice_fusion.5
  9.2 0.0 reduce-scatter.2.cloned.1.call-start
  9.2 0.5 copy.10
  9.8 0.1 broadcast_in_dim.20
  9.9 0.1 convert_element_type.43
  10.0 0.1 bitcast_multiply_fusion
  10.1 0.1 constant_dynamic-slice_fusion.1
  10.3 2.3 %all_gather.13 = bf16[512,512]{0,1:T(8,128)(2,1)S(1)} all-gather(bf16[256,512]{0,1:T(8,128)(2,1)S(1)} %pad_maximum_fusion), channel_id=1, replica_groups=mesh['layer'=4,'row'=2,'col'=4] {'row'}, dimensions={0}, use_global_device_ids=true | all-gather | bytes 786432 | tf_op jit(solution)/shard_map/all_gather | solution.py:30
  12.5 27.4 %all-gather.3.cloned.1.call-done = bf16[1024,512]{0,1:T(8,128)(2,1)} async-done(((bf16[1024,128]{0,1:T(8,128)(2,1)}), bf16[1024,512]{0,1:T(8,128)(2,1)}) %all-gather.3.cloned.1.call-update) | async-done | bytes 1048592 | tf_op jit(solution)/shard_map/all_gather | solution.py:36
  40.0 3.3 %fusion.2 = f32[1024,512]{0,1:T(8,128)} fusion(bf16[512,512]{0,1:T(8,128)(2,1)S(1)} %all_gather.13, bf16[1024,512]{0,1:T(8,128)(2,1)} %all-gather.3.cloned.1.call-done), kind=kOutput, calls=%fused_computation.13 | convolution fusion | flops 536870912 | bytes 3670016 | tf_op jit(solution)/shard_map/dot_general | solution.py:35
  43.3 0.0 all-gather.5.cloned.1.call-start
  43.3 0.7 fusion
  44.0 0.1 broadcast_in_dim.22
  44.1 0.1 convert_element_type.47
  44.2 33.9 %reduce-scatter.2.cloned.1.call-done = f32[1024,128]{0,1:T(8,128)} async-done(((f32[1024,512]{0,1:T(8,128)}), f32[1024,128]{0,1:T(8,128)}) %reduce-scatter.2.cloned.1.call-update) | async-done | bytes 524304 | tf_op jit(solution)/shard_map/reduce_scatter | solution.py:38
  78.1 1.8 bitcast_multiply_fusion.2
  80.0 2.2 %all_gather.15 = bf16[512,512]{0,1:T(8,128)(2,1)S(1)} all-gather(bf16[256,512]{0,1:T(8,128)(2,1)S(1)} %pad_maximum_fusion.1), channel_id=1, replica_groups=mesh['layer'=4,'row'=2,'col'=4] {'row'}, dimensions={0}, use_global_device_ids=true | all-gather | bytes 786432 | tf_op jit(solution)/shard_map/all_gather | solution.py:41
  82.2 25.9 %all-gather.5.cloned.1.call-done = bf16[1024,512]{0,1:T(8,128)(2,1)} async-done(((bf16[1024,128]{0,1:T(8,128)(2,1)}), bf16[1024,512]{0,1:T(8,128)(2,1)}) %all-gather.5.cloned.1.call-update) | async-done | bytes 1048592 | tf_op jit(solution)/shard_map/all_gather | solution.py:46
  108.0 2.0 %fusion.1 = f32[1024,512]{1,0:T(8,128)S(1)} fusion(bf16[1024,512]{0,1:T(8,128)(2,1)} %all-gather.5.cloned.1.call-done, bf16[512,512]{0,1:T(8,128)(2,1)S(1)} %all_gather.15), kind=kOutput, calls=%fused_computation.12 | convolution fusion | flops 536870912 | bytes 3670016 | tf_op jit(solution)/shard_map/dot_general | solution.py:45
  110.0 75.1 %all-reduce.1 = bf16[1024,512]{1,0:T(8,128)(2,1)} all-reduce(f32[1024,512]{1,0:T(8,128)S(1)} %fusion.1), channel_id=1, replica_groups=mesh['layer'=4,'row'=2,'col'=4] {'layer'}, use_global_device_ids=true, to_apply=%region_1.0 | all-reduce | flops 524288 | bytes 3145728 | tf_op jit(solution)/shard_map/psum | solution.py:48
  (14 shorter events, 0.1 us)
Async XLA Ops:
  6.5 1.6 copy-start.1
  6.5 33.4 %all-gather.3.cloned.1.call-start = ((), (), s32[]{:S(2)}) async-start(), calls=%async_computation.1 | async-start | bytes 1310720 | tf_op jit(solution)/shard_map/all_gather | solution.py:36
  6.5 2.7 %copy-start = (bf16[1024,512]{1,0:T(8,128)(2,1)S(1)}, bf16[1024,512]{1,0:T(8,128)(2,1)}, u32[]{:S(2)}) copy-start(bf16[1024,512]{1,0:T(8,128)(2,1)} %param.6) | copy-start | bytes 3145732
  8.3 1.5 copy-start.2
  9.2 68.9 %reduce-scatter.2.cloned.1.call-start = ((), (), s32[]{:S(2)}) async-start(), calls=%async_computation.2 | async-start | bytes 2621440 | tf_op jit(solution)/shard_map/reduce_scatter | solution.py:38
  43.3 64.7 %all-gather.5.cloned.1.call-start = ((), (), s32[]{:S(2)}) async-start(), calls=%async_computation.3 | async-start | bytes 1310720 | tf_op jit(solution)/shard_map/all_gather | solution.py:46
Sparse Core Ops, SparseCore 0:
  9.3 30.6 all-gather.2
  43.4 34.6 reduce-scatter.1
  80.1 27.9 all-gather.4
where the time goes:
time: 192 us
  waiting for transfers between devices  87.3 us (45%)
  blocking collectives  79.6 us (41%)
  between operations  13.2 us (7%)
  matrix products  5.27 us (3%)
  local copies, waits for them, and re-layouts  3.52 us (2%)
  other arithmetic  2.7 us (1%)
    psum x1, blocking collectives, local(): weighted = lax.psum(partial_w, 'layer').astype(jnp.bfloat16)  75.1 us
    reduce_scatter x1, waiting for transfers between devices, local(): lax.psum_scatter(partial_q, 'layer', scatter_dimension=1, tiled=True)  33.9 us
    all_gather x1, waiting for transfers between devices, local(): lax.all_gather(p_share, 'col', axis=1, tiled=True)  27.4 us
    all_gather x1, waiting for transfers between devices, local(): lax.all_gather(product, 'col', axis=1, tiled=True)  25.9 us
  transfers between devices with their start and end apart: 3, of which 3 were waited for; matrix products, arithmetic and copies ran while one was open for 1% of the time, Pallas kernels for 0%

commit v1 on v0

v1 whole, which is shorter than its diff:
```python
import functools

import jax
import jax.numpy as jnp
from jax import lax
from jax.experimental import pallas as pl
from jax.experimental.pallas import tpu as pltpu
from jax.sharding import PartitionSpec as P

BS = 64
BF = jnp.bfloat16
F32 = jnp.float32


def kernel(L, R, Z, nc, p_hbm, h_hbm, pm_ref, hm_ref, fm_ref, out_ref,
           p_in, h_in, em, pg, qg, hg, pc, in_sem, zs, zr, hs, hr, cs, cr_sem, ws, wr):
    l, r, c = lax.axis_index("layer"), lax.axis_index("row"), lax.axis_index("col")
    tr, tc = p_in.shape
    lr = tr // L
    ch = lr // nc
    G = tr // tc
    nb, lb = tr // BS, lr // BS
    lrow = pl.multiple_of(l * lr, lr)

    first = pltpu.make_async_copy(
        p_hbm.at[pl.ds(lrow, lr)], pg.at[c], in_sem.at[0])
    whole_p = pltpu.make_async_copy(p_hbm, p_in, in_sem.at[1])
    whole_h = pltpu.make_async_copy(h_hbm, h_in, in_sem.at[2])
    first.start()
    whole_h.start()
    whole_p.start()

    barrier = pltpu.get_barrier_semaphore()

    def greet(dev):
        pl.semaphore_signal(barrier, inc=1, device_id=dev)

    @pl.when(c > 0)
    def _():
        greet({"col": c - 1})

    @pl.when(c < Z - 1)
    def _():
        greet({"col": c + 1})

    for j in range(1, R):
        greet({"row": lax.rem(r + j, R)})
    for j in range(1, L):
        greet({"layer": lax.rem(l + j, L)})

    spread = (lax.broadcasted_iota(jnp.int32, (tc // BS, tc), 1) // BS
              == lax.broadcasted_iota(jnp.int32, (tc // BS, tc), 0))
    spread = spread.astype(F32).astype(BF)
    for i, m in enumerate((pm_ref, hm_ref, fm_ref)):
        em[i] = jnp.dot(m[...].astype(F32).astype(BF), spread, preferred_element_type=F32)

    def z_copy(buf, ph, k, side, origin, hop):
        view = buf.at[origin, pl.ds(k * ch, ch)]
        to = c + 1 if side == 0 else c - 1
        return pltpu.make_async_remote_copy(
            view, view, zs.at[ph, side, k, hop], zr.at[ph, side, k, hop],
            device_id={"col": to})

    def z_origin(side, d):
        return c - d if side == 0 else c + d

    def z_sends(side, d):
        there = c < Z - 1 if side == 0 else c > 0
        if d == 0:
            return there
        return there & (c >= d if side == 0 else c + d < Z)

    def z_send(buf, ph, k, d):
        for side in range(2):
            @pl.when(z_sends(side, d))
            def _():
                z_copy(buf, ph, k, side, z_origin(side, d), d).start()

    def z_step(buf, ph, k, d):
        for side in range(2):
            @pl.when(c >= d if side == 0 else c + d < Z)
            def _():
                z_copy(buf, ph, k, side, z_origin(side, d), d - 1).wait_recv()
        if d < Z - 1:
            z_send(buf, ph, k, d)

    def z_drain(buf, ph, k):
        for d in range(Z - 1):
            for side in range(2):
                @pl.when(z_sends(side, d))
                def _():
                    z_copy(buf, ph, k, side, z_origin(side, d), d).wait_send()

    def mask_chunk(k):
        for i in range(ch // BS):
            at = k * (ch // BS) + i
            keep = em[0, pl.ds(l * lb + at, 1), :].astype(BF)
            rows = pl.ds(at * BS, BS)
            pg[c, rows, :] = pg[c, rows, :] * keep

    first.wait()
    mask_chunk(0)
    near = jnp.where(c > 0, 1, 0) + jnp.where(c < Z - 1, 1, 0)
    pl.semaphore_wait(barrier, near + (R - 1) + (L - 1))
    z_send(pg, 0, 0, 0)

    def fill(src, dst, e):
        per = tc // BS

        def body(i, carry):
            keep = em[e, pl.ds(i, 1), :].astype(BF)
            dst[r * G + i // per, pl.ds(pl.multiple_of((i % per) * BS, BS), BS), :] = (
                src[pl.ds(pl.multiple_of(i * BS, BS), BS), :] * keep)
            return carry

        lax.fori_loop(0, nb, body, 0)

    def row_copy(buf, ss, rs, j, owner):
        view = buf.at[pl.ds(owner * G, G)]
        return pltpu.make_async_remote_copy(
            view, view, ss.at[j - 1], rs.at[j - 1], device_id={"row": lax.rem(r + j, R)})

    whole_h.wait()
    fill(h_in, hg, 1)
    for j in range(1, R):
        row_copy(hg, hs, hr, j, r).start()
    for k in range(1, nc):
        mask_chunk(k)
        if k == 1:
            z_send(pg, 0, 1, 0)
    whole_p.wait()
    fill(p_in, pc, 0)
    for j in range(1, R):
        row_copy(pc, cs, cr_sem, j, r).start()

    def product(left, right, k):
        def body(o, acc):
            return acc + jnp.dot(left[o, pl.ds(k * ch, ch), :], right[o],
                                 preferred_element_type=F32)

        return lax.fori_loop(0, Z, body, jnp.zeros((ch, tc), F32), unroll=Z if Z <= 4 else 1)

    def w_copy(k, j, owner):
        view = out_ref.at[pl.ds(pl.multiple_of(owner * lr + k * ch, ch), ch)]
        return pltpu.make_async_remote_copy(
            view, view, ws.at[j - 1, k], wr.at[j - 1, k],
            device_id={"layer": lax.rem(l + j, L)})

    for k in range(nc + 1):
        if 1 <= k < nc - 1:
            z_send(pg, 0, k + 1, 0)
        for d in range(1, Z):
            if k < nc:
                z_step(pg, 0, k, d)
            if k > 0:
                z_step(qg, 1, k - 1, d)
        if k < nc:
            if k == 0:
                for j in range(1, R):
                    row_copy(hg, hs, hr, j, lax.rem(r + R - j, R)).wait_recv()
            total = product(pg, hg, k)
            for i in range(ch // BS):
                at = k * (ch // BS) + i
                keep = em[2, pl.ds(l * lb + at, 1), :].astype(BF)
                qg[c, pl.ds(at * BS, BS), :] = total[i * BS:(i + 1) * BS].astype(BF) * keep
            z_send(qg, 1, k, 0)
        if k > 0:
            if k == 1:
                for j in range(1, R):
                    row_copy(pc, cs, cr_sem, j, lax.rem(r + R - j, R)).wait_recv()
            out_ref[pl.ds(pl.multiple_of(l * lr + (k - 1) * ch, ch), ch), :] = (
                product(qg, pc, k - 1).astype(BF))
            for j in range(1, L):
                w_copy(k - 1, j, l).start()

    for k in range(nc):
        z_drain(pg, 0, k)
        z_drain(qg, 1, k)
    for j in range(1, R):
        row_copy(hg, hs, hr, j, r).wait_send()
        row_copy(pc, cs, cr_sem, j, r).wait_send()
    for k in range(nc):
        for j in range(1, L):
            w_copy(k, j, l).wait_send()
            w_copy(k, j, lax.rem(l + L - j, L)).wait_recv()


def solution(mesh):
    L, R, Z = mesh.shape["layer"], mesh.shape["row"], mesh.shape["col"]
    nc = 4 if Z <= 4 else 2

    def local(density, hamiltonian, density_mask, hamilton_mask, filter_mask):
        tr, tc = density.shape
        lr = tr // L
        vmem = pl.BlockSpec(memory_space=pltpu.VMEM)
        hbm = pl.BlockSpec(memory_space=pl.ANY)
        dma = pltpu.SemaphoreType.DMA
        return pl.pallas_call(
            functools.partial(kernel, L, R, Z, nc),
            out_shape=jax.ShapeDtypeStruct((tr, tc), BF),
            in_specs=[hbm, hbm, vmem, vmem, vmem],
            out_specs=vmem,
            scratch_shapes=[
                pltpu.VMEM((tr, tc), BF),
                pltpu.VMEM((tr, tc), BF),
                pltpu.VMEM((3, tr // BS, tc), F32),
                pltpu.VMEM((Z, lr, tc), BF),
                pltpu.VMEM((Z, lr, tc), BF),
                pltpu.VMEM((R * tr // tc, tc, tc), BF),
                pltpu.VMEM((R * tr // tc, tc, tc), BF),
                dma((3,)),
                dma((2, 2, nc, Z - 1)),
                dma((2, 2, nc, Z - 1)),
                dma((R - 1,)),
                dma((R - 1,)),
                dma((R - 1,)),
                dma((R - 1,)),
                dma((L - 1, nc)),
                dma((L - 1, nc)),
            ],
            compiler_params=pltpu.CompilerParams(
                collective_id=0, has_side_effects=True, vmem_limit_bytes=52 * 2**20),
            cost_estimate=pl.CostEstimate(
                flops=4 * lr * tc * tc * Z, bytes_accessed=6 * tr * tc, transcendentals=0),
        )(density, hamiltonian, density_mask, hamilton_mask, filter_mask)

    placed = (P("row", "col"),) * 5
    return jax.shard_map(
        local, mesh=mesh, in_specs=placed, out_specs=P("row", "col"), check_vma=False)
```

time: 192 us -> 67.1 us (0.35)
  waiting for transfers between devices: 87.3 us -> 0 us
  blocking collectives: 79.6 us -> 0 us
  Pallas kernels: 0 us -> 64.4 us
  between operations: 13.2 us -> 0.01 us
  matrix products: 5.27 us -> 0 us
  other arithmetic: 2.7 us -> 0 us
    psum x1 -> x0, blocking collectives: 75.1 us -> none  [local(): weighted = lax.psum(partial_w, 'layer').astype(jnp.bfloat16)]
    pallas_call x0 -> x1, Pallas kernels: none -> 64.4 us  [local(): pl.pallas_call(functools.partial(kernel, L, R, Z, nc), out_shape=jax.Shap...]
    all_gather x2 -> x0, waiting for transfers between devices: 53.3 us -> none  [the longest x1 27.4 us: local(): lax.all_gather(p_share, 'col', axis=1, tiled=True)]
    reduce_scatter x1 -> x0, waiting for transfers between devices: 33.9 us -> none  [local(): lax.psum_scatter(partial_q, 'layer', scatter_dimension=1, tiled=True)]
    dot_general x2 -> x0, matrix products: 5.27 us -> none  [the longest x1 3.29 us: local(): jnp.dot(lax.all_gather(p_share, 'col', axis=1, tiled=True), rows, preferr...]
    all_gather x2 -> x0, blocking collectives: 4.44 us -> none  [the longest x1 2.26 us: local(): lax.all_gather(inner_rows(masked_h, groups, width, layer_pos), 'row', axi...]
    mul x3 -> x0, other arithmetic: 1.93 us -> none  [the longest x1 1.77 us: local(): product = summed_q.astype(jnp.bfloat16) * expand_mask(filter_share)]
  transfers between devices with their start and end apart: 3 -> 0, of which waited for: 3 -> 0; matrix products, arithmetic and copies ran while one was open for 1% -> 0% of each run, Pallas kernels for 0% -> 0%
where the time goes in v1:
time: 67.1 us; the launch traced here: 66.9 us
  Pallas kernels  64.4 us (96%)
  local copies, waits for them, and re-layouts  2.5 us (4%)
    pallas_call x1, Pallas kernels, local(): pl.pallas_call(functools.partial(kernel, L, R, Z, nc), out_shape=jax.Shap...  64.4 us
    unnamed x8, local copies, waits for them, and re-layouts  2.5 us

profile of v1, /device:TPU:0, one launch (start us, length us, event | category | flops | bytes accessed | tf_op | source)
XLA Modules:
  0.0 66.9 jit_solution(17315134301357091327)
XLA Ops:
  0.0 0.0 copy-start
  0.0 0.8 %copy.6.pm_ref = s32[16,8]{1,0:T(8,128)S(1)} copy(s32[16,8]{0,1:T(8,128)} %param.7) | data formatting | bytes 1024 | tf_op args[2]
  0.8 0.0 copy-done
  0.8 0.0 copy-start.1
  0.8 0.1 copy.7.hm_ref
  0.8 0.6 copy-done.1
  1.5 0.1 copy.8.fm_ref
  1.5 64.4 %shard_map.55 = bf16[1024,512]{1,0:T(8,128)(2,1)S(1)} custom-call(bf16[1024,512]{1,0:T(8,128)(2,1)} %p_hbm.1, bf16[1024,512]{1,0:T(8,128)(2,1)} %h_hbm.1, s32[16,8]{1,0:T(8,128)S(1)} %copy.6.pm_ref, s32[16,8]{1,0:T(8,128)S(1)} %copy.7.hm_ref, s32[16,8]{1,0:T(8,128)S(1)} %copy.8.fm_ref), custom_call_target="tpu_custom_call" | custom-call | flops 1073741824 | bytes 3145728 | tf_op jit(solution)/shard_map/pallas_call | solution.py:198
  65.9 1.0 %copy.10 = bf16[1024,512]{1,0:T(8,128)(2,1)} copy(bf16[1024,512]{1,0:T(8,128)(2,1)S(1)} %shard_map.55) | data formatting | bytes 2097152
Async XLA Ops:
  0.0 0.8 %copy-start = (s32[16,8]{0,1:T(8,128)S(1)}, s32[16,8]{0,1:T(8,128)}, u32[]{:S(2)}) copy-start(s32[16,8]{0,1:T(8,128)} %param.8) | copy-start | bytes 1540
  0.8 0.7 %copy-start.1 = (s32[16,8]{0,1:T(8,128)S(1)}, s32[16,8]{0,1:T(8,128)}, u32[]{:S(2)}) copy-start(s32[16,8]{0,1:T(8,128)} %param.9) | copy-start | bytes 1540

commit v2 on v1

--- a/solution.py
+++ b/solution.py
@@ -12,8 +12,8 @@
 F32 = jnp.float32
 
 
-def kernel(L, R, Z, nc, p_hbm, h_hbm, pm_ref, hm_ref, fm_ref, out_ref,
-           p_in, h_in, em, pg, qg, hg, pc, in_sem, zs, zr, hs, hr, cs, cr_sem, ws, wr):
+def kernel(L, R, Z, nc, p_hbm, h_hbm, pm_hbm, hm_hbm, fm_hbm, out_ref,
+           p_in, h_in, m_in, em, acc, pg, qg, hg, pc, in_sem, zs, zr, hs, hr, cs, cr_sem, ws, wr):
     l, r, c = lax.axis_index("layer"), lax.axis_index("row"), lax.axis_index("col")
     tr, tc = p_in.shape
     lr = tr // L
@@ -26,6 +26,10 @@
         p_hbm.at[pl.ds(lrow, lr)], pg.at[c], in_sem.at[0])
     whole_p = pltpu.make_async_copy(p_hbm, p_in, in_sem.at[1])
     whole_h = pltpu.make_async_copy(h_hbm, h_in, in_sem.at[2])
+    masks = [pltpu.make_async_copy(m, m_in.at[i], in_sem.at[3 + i])
+             for i, m in enumerate((pm_hbm, hm_hbm, fm_hbm))]
+    for m in masks:
+        m.start()
     first.start()
     whole_h.start()
     whole_p.start()
@@ -51,8 +55,11 @@
     spread = (lax.broadcasted_iota(jnp.int32, (tc // BS, tc), 1) // BS
               == lax.broadcasted_iota(jnp.int32, (tc // BS, tc), 0))
     spread = spread.astype(F32).astype(BF)
-    for i, m in enumerate((pm_ref, hm_ref, fm_ref)):
-        em[i] = jnp.dot(m[...].astype(F32).astype(BF), spread, preferred_element_type=F32)
+    for i in range(3):
+        masks[i].wait()
+        em[i] = lax.dot_general(
+            m_in[i].astype(F32).astype(BF), spread, (((0,), (0,)), ((), ())),
+            preferred_element_type=F32)
 
     def z_copy(buf, ph, k, side, origin, hop):
         view = buf.at[origin, pl.ds(k * ch, ch)]
@@ -99,10 +106,12 @@
             pg[c, rows, :] = pg[c, rows, :] * keep
 
     first.wait()
-    mask_chunk(0)
     near = jnp.where(c > 0, 1, 0) + jnp.where(c < Z - 1, 1, 0)
-    pl.semaphore_wait(barrier, near + (R - 1) + (L - 1))
-    z_send(pg, 0, 0, 0)
+    for k in range(nc):
+        mask_chunk(k)
+        if k == 0:
+            pl.semaphore_wait(barrier, near + (R - 1) + (L - 1))
+        z_send(pg, 0, k, 0)
 
     def fill(src, dst, e):
         per = tc // BS
@@ -124,21 +133,20 @@
     fill(h_in, hg, 1)
     for j in range(1, R):
         row_copy(hg, hs, hr, j, r).start()
-    for k in range(1, nc):
-        mask_chunk(k)
-        if k == 1:
-            z_send(pg, 0, 1, 0)
     whole_p.wait()
     fill(p_in, pc, 0)
     for j in range(1, R):
         row_copy(pc, cs, cr_sem, j, r).start()
 
-    def product(left, right, k):
-        def body(o, acc):
-            return acc + jnp.dot(left[o, pl.ds(k * ch, ch), :], right[o],
-                                 preferred_element_type=F32)
-
-        return lax.fori_loop(0, Z, body, jnp.zeros((ch, tc), F32), unroll=Z if Z <= 4 else 1)
+    def begin(left, right, rows):
+        acc[rows, :] = jnp.dot(left[c, rows, :], right[c], preferred_element_type=F32)
+
+    def add(left, right, rows, d):
+        for side in range(2):
+            @pl.when(c >= d if side == 0 else c + d < Z)
+            def _():
+                o = z_origin(side, d)
+                acc[rows, :] += jnp.dot(left[o, rows, :], right[o], preferred_element_type=F32)
 
     def w_copy(k, j, owner):
         view = out_ref.at[pl.ds(pl.multiple_of(owner * lr + k * ch, ch), ch)]
@@ -146,32 +154,36 @@
             view, view, ws.at[j - 1, k], wr.at[j - 1, k],
             device_id={"layer": lax.rem(l + j, L)})
 
-    for k in range(nc + 1):
-        if 1 <= k < nc - 1:
-            z_send(pg, 0, k + 1, 0)
+    everything = pl.ds(0, lr)
+    for d in range(1, Z - 1):
+        for k in range(nc):
+            z_step(pg, 0, k, d)
+        if d == 1:
+            for j in range(1, R):
+                row_copy(hg, hs, hr, j, lax.rem(r + R - j, R)).wait_recv()
+            begin(pg, hg, everything)
+        add(pg, hg, everything, d)
+    for k in range(nc):
+        z_step(pg, 0, k, Z - 1)
+        add(pg, hg, pl.ds(k * ch, ch), Z - 1)
+        for i in range(ch // BS):
+            at = k * (ch // BS) + i
+            rows = pl.ds(at * BS, BS)
+            keep = em[2, pl.ds(l * lb + at, 1), :].astype(BF)
+            qg[c, rows, :] = acc[rows, :].astype(BF) * keep
+        z_send(qg, 1, k, 0)
+
+    for j in range(1, R):
+        row_copy(pc, cs, cr_sem, j, lax.rem(r + R - j, R)).wait_recv()
+    for k in range(nc):
+        rows = pl.ds(k * ch, ch)
+        begin(qg, pc, rows)
         for d in range(1, Z):
-            if k < nc:
-                z_step(pg, 0, k, d)
-            if k > 0:
-                z_step(qg, 1, k - 1, d)
-        if k < nc:
-            if k == 0:
-                for j in range(1, R):
-                    row_copy(hg, hs, hr, j, lax.rem(r + R - j, R)).wait_recv()
-            total = product(pg, hg, k)
-            for i in range(ch // BS):
-                at = k * (ch // BS) + i
-                keep = em[2, pl.ds(l * lb + at, 1), :].astype(BF)
-                qg[c, pl.ds(at * BS, BS), :] = total[i * BS:(i + 1) * BS].astype(BF) * keep
-            z_send(qg, 1, k, 0)
-        if k > 0:
-            if k == 1:
-                for j in range(1, R):
-                    row_copy(pc, cs, cr_sem, j, lax.rem(r + R - j, R)).wait_recv()
-            out_ref[pl.ds(pl.multiple_of(l * lr + (k - 1) * ch, ch), ch), :] = (
-                product(qg, pc, k - 1).astype(BF))
-            for j in range(1, L):
-                w_copy(k - 1, j, l).start()
+            z_step(qg, 1, k, d)
+            add(qg, pc, rows, d)
+        out_ref[pl.ds(pl.multiple_of(l * lr + k * ch, ch), ch), :] = acc[rows, :].astype(BF)
+        for j in range(1, L):
+            w_copy(k, j, l).start()
 
     for k in range(nc):
         z_drain(pg, 0, k)
@@ -198,17 +210,19 @@
         return pl.pallas_call(
             functools.partial(kernel, L, R, Z, nc),
             out_shape=jax.ShapeDtypeStruct((tr, tc), BF),
-            in_specs=[hbm, hbm, vmem, vmem, vmem],
+            in_specs=[hbm] * 5,
             out_specs=vmem,
             scratch_shapes=[
                 pltpu.VMEM((tr, tc), BF),
                 pltpu.VMEM((tr, tc), BF),
+                pltpu.VMEM((3, tc // BS, tr // BS), jnp.int32),
                 pltpu.VMEM((3, tr // BS, tc), F32),
+                pltpu.VMEM((lr, tc), F32),
                 pltpu.VMEM((Z, lr, tc), BF),
                 pltpu.VMEM((Z, lr, tc), BF),
                 pltpu.VMEM((R * tr // tc, tc, tc), BF),
                 pltpu.VMEM((R * tr // tc, tc, tc), BF),
-                dma((3,)),
+                dma((6,)),
                 dma((2, 2, nc, Z - 1)),
                 dma((2, 2, nc, Z - 1)),
                 dma((R - 1,)),
@@ -222,7 +236,7 @@
                 collective_id=0, has_side_effects=True, vmem_limit_bytes=52 * 2**20),
             cost_estimate=pl.CostEstimate(
                 flops=4 * lr * tc * tc * Z, bytes_accessed=6 * tr * tc, transcendentals=0),
-        )(density, hamiltonian, density_mask, hamilton_mask, filter_mask)
+        )(density, hamiltonian, density_mask.T, hamilton_mask.T, filter_mask.T)
 
     placed = (P("row", "col"),) * 5
     return jax.shard_map(

time: 67.1 us -> 50.7 us (0.76)
  Pallas kernels: 64.4 us -> 47.4 us
    pallas_call x1, Pallas kernels: 64.4 us -> 47.4 us  [local(): pl.pallas_call(functools.partial(kernel, L, R, Z, nc), out_shape=jax.Shap...]
    unnamed x8 -> x7, local copies, waits for them, and re-layouts: 2.5 us -> 3.03 us
where the time goes in v2:
time: 50.7 us; the launch traced here: 50.5 us
  Pallas kernels  47.4 us (93%)
  local copies, waits for them, and re-layouts  3.03 us (6%)
    pallas_call x1, Pallas kernels, local(): pl.pallas_call(functools.partial(kernel, L, R, Z, nc), out_shape=jax.Shap...  47.4 us
    unnamed x7, local copies, waits for them, and re-layouts  3.03 us

profile of v2, /device:TPU:0, one launch (start us, length us, event | category | flops | bytes accessed | tf_op | source)
XLA Modules:
  0.0 50.5 jit_solution(4934639058888419486)
XLA Ops:
  0.0 0.0 copy-start
  0.0 0.7 %copy-done = s32[16,8]{0,1:T(8,128)S(1)} copy-done((s32[16,8]{0,1:T(8,128)S(1)}, s32[16,8]{0,1:T(8,128)}, u32[]{:S(2)}) %copy-start) | copy-done | bytes 536
  0.7 0.0 copy-start.1
  0.7 0.7 %copy-done.1 = s32[16,8]{0,1:T(8,128)S(1)} copy-done((s32[16,8]{0,1:T(8,128)S(1)}, s32[16,8]{0,1:T(8,128)}, u32[]{:S(2)}) %copy-start.1) | copy-done | bytes 536
  1.4 0.0 copy-start.2
  1.4 0.7 %copy-done.2 = s32[16,8]{0,1:T(8,128)S(1)} copy-done((s32[16,8]{0,1:T(8,128)S(1)}, s32[16,8]{0,1:T(8,128)}, u32[]{:S(2)}) %copy-start.2) | copy-done | bytes 536
  2.1 47.4 %shard_map.55 = bf16[1024,512]{1,0:T(8,128)(2,1)S(1)} custom-call(bf16[1024,512]{1,0:T(8,128)(2,1)} %p_hbm.1, bf16[1024,512]{1,0:T(8,128)(2,1)} %h_hbm.1, s32[8,16]{1,0:T(8,128)S(1)} %bitcast.3, s32[8,16]{1,0:T(8,128)S(1)} %bitcast.4, s32[8,16]{1,0:T(8,128)S(1)} %bitcast.5), custom_call_target="tpu_custom_call" | custom-call | flops 1073741824 | bytes 3145728 | tf_op jit(solution)/shard_map/pallas_call | solution.py:210
  49.5 1.0 %copy.7 = bf16[1024,512]{1,0:T(8,128)(2,1)} copy(bf16[1024,512]{1,0:T(8,128)(2,1)S(1)} %shard_map.55) | data formatting | bytes 2097152
Async XLA Ops:
  0.0 0.7 %copy-start = (s32[16,8]{0,1:T(8,128)S(1)}, s32[16,8]{0,1:T(8,128)}, u32[]{:S(2)}) copy-start(s32[16,8]{0,1:T(8,128)} %param.7) | copy-start | bytes 1540
  0.7 0.7 %copy-start.1 = (s32[16,8]{0,1:T(8,128)S(1)}, s32[16,8]{0,1:T(8,128)}, u32[]{:S(2)}) copy-start(s32[16,8]{0,1:T(8,128)} %param.8) | copy-start | bytes 1540
  1.4 0.7 %copy-start.2 = (s32[16,8]{0,1:T(8,128)S(1)}, s32[16,8]{0,1:T(8,128)}, u32[]{:S(2)}) copy-start(s32[16,8]{0,1:T(8,128)} %param.9) | copy-start | bytes 1540

commit v3 on v2

--- a/solution.py
+++ b/solution.py
@@ -13,7 +13,8 @@
 
 
 def kernel(L, R, Z, nc, p_hbm, h_hbm, pm_hbm, hm_hbm, fm_hbm, out_ref,
-           p_in, h_in, m_in, em, acc, pg, qg, hg, pc, in_sem, zs, zr, hs, hr, cs, cr_sem, ws, wr):
+           p_in, h_in, m_in, em, acc, pg, qg, hg, pc, in_sem, zs, zr, hs, hr, cs, cr_sem, ws, wr,
+           acc_e=None, pe=None, we=None, gs=None, gr=None, fs=None, fr=None, es=None, er=None):
     l, r, c = lax.axis_index("layer"), lax.axis_index("row"), lax.axis_index("col")
     tr, tc = p_in.shape
     lr = tr // L
@@ -21,6 +22,9 @@
     G = tr // tc
     nb, lb = tr // BS, lr // BS
     lrow = pl.multiple_of(l * lr, lr)
+    helped = acc_e is not None
+    middle = (c > 0) & (c < Z - 1)
+    end = jnp.where(c <= 1, 0, Z - 1)
 
     first = pltpu.make_async_copy(
         p_hbm.at[pl.ds(lrow, lr)], pg.at[c], in_sem.at[0])
@@ -71,21 +75,26 @@
     def z_origin(side, d):
         return c - d if side == 0 else c + d
 
-    def z_sends(side, d):
-        there = c < Z - 1 if side == 0 else c > 0
+    def z_sends(ph, side, d):
+        last = 1 if helped and ph == 1 else 0
+        there = c < Z - 1 - last if side == 0 else c > last
         if d == 0:
             return there
         return there & (c >= d if side == 0 else c + d < Z)
 
+    def z_gets(ph, side, d):
+        got = c >= d if side == 0 else c + d < Z
+        return got & middle if helped and ph == 1 else got
+
     def z_send(buf, ph, k, d):
         for side in range(2):
-            @pl.when(z_sends(side, d))
+            @pl.when(z_sends(ph, side, d))
             def _():
                 z_copy(buf, ph, k, side, z_origin(side, d), d).start()
 
     def z_step(buf, ph, k, d):
         for side in range(2):
-            @pl.when(c >= d if side == 0 else c + d < Z)
+            @pl.when(z_gets(ph, side, d))
             def _():
                 z_copy(buf, ph, k, side, z_origin(side, d), d - 1).wait_recv()
         if d < Z - 1:
@@ -94,7 +103,7 @@
     def z_drain(buf, ph, k):
         for d in range(Z - 1):
             for side in range(2):
-                @pl.when(z_sends(side, d))
+                @pl.when(z_sends(ph, side, d))
                 def _():
                     z_copy(buf, ph, k, side, z_origin(side, d), d).wait_send()
 
@@ -141,12 +150,34 @@
     def begin(left, right, rows):
         acc[rows, :] = jnp.dot(left[c, rows, :], right[c], preferred_element_type=F32)
 
-    def add(left, right, rows, d):
+    def add(ph, left, right, rows, d):
         for side in range(2):
-            @pl.when(c >= d if side == 0 else c + d < Z)
+            @pl.when(z_gets(ph, side, d))
             def _():
                 o = z_origin(side, d)
                 acc[rows, :] += jnp.dot(left[o, rows, :], right[o], preferred_element_type=F32)
+                if helped and ph == 1:
+                    acc_e[...] += jnp.dot(left[o, rows, :], pe[o], preferred_element_type=F32)
+
+    def share(row, layer):
+        start = layer * lr
+        return pe.at[row * G + start // tc, pl.ds(pl.multiple_of(start % tc, lr), lr)]
+
+    def share_copy(j, layer):
+        return pltpu.make_async_remote_copy(
+            share(r, layer), share(r, layer), gs.at[j - 1], gr.at[j - 1],
+            device_id={"layer": lax.rem(l + j, L)})
+
+    def pass_copy(q, i, row, layer):
+        return pltpu.make_async_remote_copy(
+            share(row, layer), share(row, layer), fs.at[q - 1, i], fr.at[q - 1, i],
+            device_id={"row": lax.rem(r + q, R)})
+
+    def end_copy(k):
+        return pltpu.make_async_remote_copy(
+            we.at[pl.ds(k * ch, ch)],
+            out_ref.at[pl.ds(pl.multiple_of(l * lr + k * ch, ch), ch)],
+            es.at[k], er.at[k], device_id={"col": jnp.where(c == 1, 0, jnp.where(c == 0, 1, jnp.where(c == Z - 1, Z - 2, Z - 1)))})
 
     def w_copy(k, j, owner):
         view = out_ref.at[pl.ds(pl.multiple_of(owner * lr + k * ch, ch), ch)]
@@ -162,10 +193,18 @@
             for j in range(1, R):
                 row_copy(hg, hs, hr, j, lax.rem(r + R - j, R)).wait_recv()
             begin(pg, hg, everything)
-        add(pg, hg, everything, d)
+            if helped:
+                @pl.when(middle)
+                def _():
+                    share(r, l)[...] = pg[end]
+                    for j in range(1, L):
+                        share_copy(j, l).start()
+                    for q in range(1, R):
+                        pass_copy(q, 0, r, l).start()
+        add(0, pg, hg, everything, d)
     for k in range(nc):
         z_step(pg, 0, k, Z - 1)
-        add(pg, hg, pl.ds(k * ch, ch), Z - 1)
+        add(0, pg, hg, pl.ds(k * ch, ch), Z - 1)
         for i in range(ch // BS):
             at = k * (ch // BS) + i
             rows = pl.ds(at * BS, BS)
@@ -175,15 +214,56 @@
 
     for j in range(1, R):
         row_copy(pc, cs, cr_sem, j, lax.rem(r + R - j, R)).wait_recv()
-    for k in range(nc):
+
+    def w_sends(k):
+        for j in range(1, L):
+            w_copy(k, j, l).start()
+
+    def last_product(k):
         rows = pl.ds(k * ch, ch)
         begin(qg, pc, rows)
+        if helped:
+            if k == 0:
+                for j in range(1, L):
+                    came = lax.rem(l + L - j, L)
+                    share_copy(j, came).wait_recv()
+                    for q in range(1, R):
+                        pass_copy(q, j, r, came).start()
+                for q in range(1, R):
+                    row = lax.rem(r + R - q, R)
+                    for j in range(L):
+                        pass_copy(q, j, row, lax.rem(l + L - j, L)).wait_recv()
+            acc_e[...] = jnp.dot(qg[c, rows, :], pe[c], preferred_element_type=F32)
         for d in range(1, Z):
             z_step(qg, 1, k, d)
-            add(qg, pc, rows, d)
+            add(1, qg, pc, rows, d)
+        if helped:
+            we[rows, :] = acc_e[...].astype(BF)
+            end_copy(k).start()
         out_ref[pl.ds(pl.multiple_of(l * lr + k * ch, ch), ch), :] = acc[rows, :].astype(BF)
-        for j in range(1, L):
-            w_copy(k, j, l).start()
+        w_sends(k)
+
+    if helped:
+        @pl.when(middle)
+        def _():
+            for k in range(nc):
+                last_product(k)
+            for k in range(nc):
+                end_copy(k).wait_send()
+            for j in range(1, L):
+                share_copy(j, l).wait_send()
+            for q in range(1, R):
+                for j in range(L):
+                    pass_copy(q, j, r, lax.rem(l + L - j, L)).wait_send()
+
+        @pl.when(jnp.logical_not(middle))
+        def _():
+            for k in range(nc):
+                end_copy(k).wait_recv()
+                w_sends(k)
+    else:
+        for k in range(nc):
+            last_product(k)
 
     for k in range(nc):
         z_drain(pg, 0, k)
@@ -205,8 +285,19 @@
         tr, tc = density.shape
         lr = tr // L
         vmem = pl.BlockSpec(memory_space=pltpu.VMEM)
-        hbm = pl.BlockSpec(memory_space=pl.ANY)
+        hbm = pl.BlockSpec(memory_space=pltpu.HBM)
         dma = pltpu.SemaphoreType.DMA
+        extra = [
+            pltpu.VMEM((lr // nc, tc), F32),
+            pltpu.VMEM((R * tr // tc, tc, tc), BF),
+            pltpu.VMEM((lr, tc), BF),
+            dma((L - 1,)),
+            dma((L - 1,)),
+            dma((R - 1, L)),
+            dma((R - 1, L)),
+            dma((nc,)),
+            dma((nc,)),
+        ] if Z == 4 else []
         return pl.pallas_call(
             functools.partial(kernel, L, R, Z, nc),
             out_shape=jax.ShapeDtypeStruct((tr, tc), BF),
@@ -231,7 +322,7 @@
                 dma((R - 1,)),
                 dma((L - 1, nc)),
                 dma((L - 1, nc)),
-            ],
+            ] + extra,
             compiler_params=pltpu.CompilerParams(
                 collective_id=0, has_side_effects=True, vmem_limit_bytes=52 * 2**20),
             cost_estimate=pl.CostEstimate(

time: 50.7 us -> 53.4 us (1.053)
  Pallas kernels: 47.4 us -> 50.2 us
    pallas_call x1, Pallas kernels: 47.4 us -> 50.2 us  [local(): pl.pallas_call(functools.partial(kernel, L, R, Z, nc), out_shape=jax.Shap...]
where the time goes in v3:
time: 53.4 us; the launch traced here: 53.2 us
  Pallas kernels  50.2 us (94%)
  local copies, waits for them, and re-layouts  3.03 us (6%)
    pallas_call x1, Pallas kernels, local(): pl.pallas_call(functools.partial(kernel, L, R, Z, nc), out_shape=jax.Shap...  50.2 us
    unnamed x7, local copies, waits for them, and re-layouts  3.03 us

profile of v3, /device:TPU:0, one launch (start us, length us, event | category | flops | bytes accessed | tf_op | source)
XLA Modules:
  0.0 53.2 jit_solution(10141972695169177167)
XLA Ops:
  0.0 0.0 copy-start
  0.0 0.7 %copy-done = s32[16,8]{0,1:T(8,128)S(1)} copy-done((s32[16,8]{0,1:T(8,128)S(1)}, s32[16,8]{0,1:T(8,128)}, u32[]{:S(2)}) %copy-start) | copy-done | bytes 536
  0.7 0.0 copy-start.1
  0.7 0.7 %copy-done.1 = s32[16,8]{0,1:T(8,128)S(1)} copy-done((s32[16,8]{0,1:T(8,128)S(1)}, s32[16,8]{0,1:T(8,128)}, u32[]{:S(2)}) %copy-start.1) | copy-done | bytes 536
  1.4 0.0 copy-start.2
  1.4 0.7 %copy-done.2 = s32[16,8]{0,1:T(8,128)S(1)} copy-done((s32[16,8]{0,1:T(8,128)S(1)}, s32[16,8]{0,1:T(8,128)}, u32[]{:S(2)}) %copy-start.2) | copy-done | bytes 536
  2.1 50.2 %shard_map.55 = bf16[1024,512]{1,0:T(8,128)(2,1)S(1)} custom-call(bf16[1024,512]{1,0:T(8,128)(2,1)} %p_hbm.1, bf16[1024,512]{1,0:T(8,128)(2,1)} %h_hbm.1, s32[8,16]{1,0:T(8,128)S(1)} %bitcast.3, s32[8,16]{1,0:T(8,128)S(1)} %bitcast.4, s32[8,16]{1,0:T(8,128)S(1)} %bitcast.5), custom_call_target="tpu_custom_call" | custom-call | flops 1073741824 | bytes 3145728 | tf_op jit(solution)/shard_map/pallas_call | solution.py:301
  52.2 1.0 %copy.7 = bf16[1024,512]{1,0:T(8,128)(2,1)} copy(bf16[1024,512]{1,0:T(8,128)(2,1)S(1)} %shard_map.55) | data formatting | bytes 2097152
Async XLA Ops:
  0.0 0.7 %copy-start = (s32[16,8]{0,1:T(8,128)S(1)}, s32[16,8]{0,1:T(8,128)}, u32[]{:S(2)}) copy-start(s32[16,8]{0,1:T(8,128)} %param.7) | copy-start | bytes 1540
  0.7 0.7 %copy-start.1 = (s32[16,8]{0,1:T(8,128)S(1)}, s32[16,8]{0,1:T(8,128)}, u32[]{:S(2)}) copy-start(s32[16,8]{0,1:T(8,128)} %param.8) | copy-start | bytes 1540
  1.4 0.7 %copy-start.2 = (s32[16,8]{0,1:T(8,128)S(1)}, s32[16,8]{0,1:T(8,128)}, u32[]{:S(2)}) copy-start(s32[16,8]{0,1:T(8,128)} %param.9) | copy-start | bytes 1540

commit v4 on v3

--- a/solution.py
+++ b/solution.py
@@ -12,9 +12,10 @@
 F32 = jnp.float32
 
 
-def kernel(L, R, Z, nc, p_hbm, h_hbm, pm_hbm, hm_hbm, fm_hbm, out_ref,
-           p_in, h_in, m_in, em, acc, pg, qg, hg, pc, in_sem, zs, zr, hs, hr, cs, cr_sem, ws, wr,
-           acc_e=None, pe=None, we=None, gs=None, gr=None, fs=None, fr=None, es=None, er=None):
+def kernel(L, R, Z, nc, p_hbm, h_hbm, m_in, out_ref,
+           p_in, h_in, em, acc, pg, qg, hg, pc, in_sem, zs, zr, hs, hr, cs, cr_sem, ws, wr,
+           acc_e=None, pe=None, we=None, gs=None, gr=None, fs=None, fr=None, es=None, er=None,
+           xs=None, xr=None):
     l, r, c = lax.axis_index("layer"), lax.axis_index("row"), lax.axis_index("col")
     tr, tc = p_in.shape
     lr = tr // L
@@ -22,6 +23,8 @@
     G = tr // tc
     nb, lb = tr // BS, lr // BS
     lrow = pl.multiple_of(l * lr, lr)
+    nw = nc // 2
+    cw = lr // nw
     helped = acc_e is not None
     middle = (c > 0) & (c < Z - 1)
     end = jnp.where(c <= 1, 0, Z - 1)
@@ -30,10 +33,6 @@
         p_hbm.at[pl.ds(lrow, lr)], pg.at[c], in_sem.at[0])
     whole_p = pltpu.make_async_copy(p_hbm, p_in, in_sem.at[1])
     whole_h = pltpu.make_async_copy(h_hbm, h_in, in_sem.at[2])
-    masks = [pltpu.make_async_copy(m, m_in.at[i], in_sem.at[3 + i])
-             for i, m in enumerate((pm_hbm, hm_hbm, fm_hbm))]
-    for m in masks:
-        m.start()
     first.start()
     whole_h.start()
     whole_p.start()
@@ -60,7 +59,6 @@
               == lax.broadcasted_iota(jnp.int32, (tc // BS, tc), 0))
     spread = spread.astype(F32).astype(BF)
     for i in range(3):
-        masks[i].wait()
         em[i] = lax.dot_general(
             m_in[i].astype(F32).astype(BF), spread, (((0,), (0,)), ((), ())),
             preferred_element_type=F32)
@@ -163,10 +161,21 @@
         start = layer * lr
         return pe.at[row * G + start // tc, pl.ds(pl.multiple_of(start % tc, lr), lr)]
 
-    def share_copy(j, layer):
-        return pltpu.make_async_remote_copy(
-            share(r, layer), share(r, layer), gs.at[j - 1], gr.at[j - 1],
-            device_id={"layer": lax.rem(l + j, L)})
+    def flip(t):
+        return (l, l + 1 - 2 * (l % 2), l + 2 - 4 * (l // 2), L - 1 - l)[t]
+
+    def share_copy(t, layer):
+        return pltpu.make_async_remote_copy(
+            share(r, layer), share(r, layer), gs.at[t - 1], gr.at[t - 1],
+            device_id={"layer": flip(t)})
+
+    beside = jnp.where(c == 1, 0, jnp.where(c == 0, 1, jnp.where(c == Z - 1, Z - 2, Z - 1)))
+
+    def far_copy():
+        start = flip(3) * lr
+        view = pc.at[r * G + start // tc, pl.ds(pl.multiple_of(start % tc, lr), lr)]
+        return pltpu.make_async_remote_copy(
+            view, share(r, flip(3)), xs.at[0], xr.at[0], device_id={"col": beside})
 
     def pass_copy(q, i, row, layer):
         return pltpu.make_async_remote_copy(
@@ -175,9 +184,9 @@
 
     def end_copy(k):
         return pltpu.make_async_remote_copy(
-            we.at[pl.ds(k * ch, ch)],
-            out_ref.at[pl.ds(pl.multiple_of(l * lr + k * ch, ch), ch)],
-            es.at[k], er.at[k], device_id={"col": jnp.where(c == 1, 0, jnp.where(c == 0, 1, jnp.where(c == Z - 1, Z - 2, Z - 1)))})
+            we.at[pl.ds(k * cw, cw)],
+            out_ref.at[pl.ds(pl.multiple_of(l * lr + k * cw, cw), cw)],
+            es.at[k], er.at[k], device_id={"col": beside})
 
     def w_copy(k, j, owner):
         view = out_ref.at[pl.ds(pl.multiple_of(owner * lr + k * ch, ch), ch)]
@@ -194,11 +203,15 @@
                 row_copy(hg, hs, hr, j, lax.rem(r + R - j, R)).wait_recv()
             begin(pg, hg, everything)
             if helped:
+                @pl.when(jnp.logical_not(middle))
+                def _():
+                    far_copy().start()
+
                 @pl.when(middle)
                 def _():
                     share(r, l)[...] = pg[end]
-                    for j in range(1, L):
-                        share_copy(j, l).start()
+                    for t in (1, 2):
+                        share_copy(t, l).start()
                     for q in range(1, R):
                         pass_copy(q, 0, r, l).start()
         add(0, pg, hg, everything, d)
@@ -215,55 +228,89 @@
     for j in range(1, R):
         row_copy(pc, cs, cr_sem, j, lax.rem(r + R - j, R)).wait_recv()
 
-    def w_sends(k):
-        for j in range(1, L):
-            w_copy(k, j, l).start()
-
-    def last_product(k):
-        rows = pl.ds(k * ch, ch)
+    def turn_copy(k, t, owner, lane):
+        view = out_ref.at[pl.ds(pl.multiple_of(owner * lr + k * ch, ch), ch)]
+        return pltpu.make_async_remote_copy(
+            view, view, ws.at[lane, k], wr.at[lane, k], device_id={"layer": flip(t)})
+
+    def via(k):
+        return 1 + k % 2
+
+    def w_sends(kw):
+        if not helped:
+            for k in (2 * kw, 2 * kw + 1):
+                for j in range(1, L):
+                    w_copy(k, j, l).start()
+            return
+        for i in range(2):
+            for t in (1, 2):
+                turn_copy(2 * kw + (i + t + 1) % 2, t, l, t - 1).start()
+        if kw > 0:
+            w_turns(kw - 1)
+
+    def w_turns(kw):
+        for k in (2 * kw, 2 * kw + 1):
+            t = via(k)
+            turn_copy(k, t, flip(t), t - 1).wait_recv()
+            turn_copy(k, 3 - t, flip(t), 2).start()
+
+    def last_product(kw):
+        rows = pl.ds(kw * cw, cw)
         begin(qg, pc, rows)
         if helped:
-            if k == 0:
-                for j in range(1, L):
-                    came = lax.rem(l + L - j, L)
-                    share_copy(j, came).wait_recv()
+            if kw == 0:
+                for t in (1, 2):
+                    share_copy(t, flip(t)).wait_recv()
                     for q in range(1, R):
-                        pass_copy(q, j, r, came).start()
+                        pass_copy(q, t, r, flip(t)).start()
+                far_copy().wait_recv()
+                for q in range(1, R):
+                    pass_copy(q, 3, r, flip(3)).start()
                 for q in range(1, R):
                     row = lax.rem(r + R - q, R)
-                    for j in range(L):
-                        pass_copy(q, j, row, lax.rem(l + L - j, L)).wait_recv()
+                    for t in range(L):
+                        pass_copy(q, t, row, flip(t)).wait_recv()
             acc_e[...] = jnp.dot(qg[c, rows, :], pe[c], preferred_element_type=F32)
         for d in range(1, Z):
-            z_step(qg, 1, k, d)
+            for k in (2 * kw, 2 * kw + 1):
+                z_step(qg, 1, k, d)
             add(1, qg, pc, rows, d)
         if helped:
             we[rows, :] = acc_e[...].astype(BF)
-            end_copy(k).start()
-        out_ref[pl.ds(pl.multiple_of(l * lr + k * ch, ch), ch), :] = acc[rows, :].astype(BF)
-        w_sends(k)
+            end_copy(kw).start()
+        out_ref[pl.ds(pl.multiple_of(l * lr + kw * cw, cw), cw), :] = acc[rows, :].astype(BF)
+        w_sends(kw)
 
     if helped:
         @pl.when(middle)
         def _():
-            for k in range(nc):
-                last_product(k)
-            for k in range(nc):
-                end_copy(k).wait_send()
-            for j in range(1, L):
-                share_copy(j, l).wait_send()
-            for q in range(1, R):
-                for j in range(L):
-                    pass_copy(q, j, r, lax.rem(l + L - j, L)).wait_send()
+            for kw in range(nw):
+                last_product(kw)
 
         @pl.when(jnp.logical_not(middle))
         def _():
-            for k in range(nc):
-                end_copy(k).wait_recv()
-                w_sends(k)
+            for kw in range(nw):
+                end_copy(kw).wait_recv()
+                w_sends(kw)
+
+        w_turns(nw - 1)
+
+        @pl.when(middle)
+        def _():
+            for kw in range(nw):
+                end_copy(kw).wait_send()
+            for t in (1, 2):
+                share_copy(t, l).wait_send()
+            for q in range(1, R):
+                for t in range(L):
+                    pass_copy(q, t, r, flip(t)).wait_send()
+
+        @pl.when(jnp.logical_not(middle))
+        def _():
+            far_copy().wait_send()
     else:
-        for k in range(nc):
-            last_product(k)
+        for kw in range(nw):
+            last_product(kw)
 
     for k in range(nc):
         z_drain(pg, 0, k)
@@ -272,6 +319,14 @@
         row_copy(hg, hs, hr, j, r).wait_send()
         row_copy(pc, cs, cr_sem, j, r).wait_send()
     for k in range(nc):
+        if helped:
+            for t in (1, 2):
+                turn_copy(k, t, l, t - 1).wait_send()
+                if t != via(k):
+                    turn_copy(k, t, flip(t), t - 1).wait_recv()
+            turn_copy(k, 3 - via(k), flip(via(k)), 2).wait_send()
+            turn_copy(k, via(k), flip(3), 2).wait_recv()
+            continue
         for j in range(1, L):
             w_copy(k, j, l).wait_send()
             w_copy(k, j, lax.rem(l + L - j, L)).wait_recv()
@@ -288,32 +343,33 @@
         hbm = pl.BlockSpec(memory_space=pltpu.HBM)
         dma = pltpu.SemaphoreType.DMA
         extra = [
-            pltpu.VMEM((lr // nc, tc), F32),
+            pltpu.VMEM((2 * lr // nc, tc), F32),
             pltpu.VMEM((R * tr // tc, tc, tc), BF),
             pltpu.VMEM((lr, tc), BF),
-            dma((L - 1,)),
-            dma((L - 1,)),
+            dma((2,)),
+            dma((2,)),
             dma((R - 1, L)),
             dma((R - 1, L)),
-            dma((nc,)),
-            dma((nc,)),
-        ] if Z == 4 else []
+            dma((nc // 2,)),
+            dma((nc // 2,)),
+            dma((1,)),
+            dma((1,)),
+        ] if Z == 4 and L == 4 else []
         return pl.pallas_call(
             functools.partial(kernel, L, R, Z, nc),
             out_shape=jax.ShapeDtypeStruct((tr, tc), BF),
-            in_specs=[hbm] * 5,
+            in_specs=[hbm, hbm, vmem],
             out_specs=vmem,
             scratch_shapes=[
                 pltpu.VMEM((tr, tc), BF),
                 pltpu.VMEM((tr, tc), BF),
-                pltpu.VMEM((3, tc // BS, tr // BS), jnp.int32),
                 pltpu.VMEM((3, tr // BS, tc), F32),
                 pltpu.VMEM((lr, tc), F32),
                 pltpu.VMEM((Z, lr, tc), BF),
                 pltpu.VMEM((Z, lr, tc), BF),
                 pltpu.VMEM((R * tr // tc, tc, tc), BF),
                 pltpu.VMEM((R * tr // tc, tc, tc), BF),
-                dma((6,)),
+                dma((3,)),
                 dma((2, 2, nc, Z - 1)),
                 dma((2, 2, nc, Z - 1)),
                 dma((R - 1,)),
@@ -327,7 +383,7 @@
                 collective_id=0, has_side_effects=True, vmem_limit_bytes=52 * 2**20),
             cost_estimate=pl.CostEstimate(
                 flops=4 * lr * tc * tc * Z, bytes_accessed=6 * tr * tc, transcendentals=0),
-        )(density, hamiltonian, density_mask.T, hamilton_mask.T, filter_mask.T)
+        )(density, hamiltonian, jnp.stack([density_mask.T, hamilton_mask.T, filter_mask.T]))
 
     placed = (P("row", "col"),) * 5
     return jax.shard_map(

time: 53.4 us -> 49.2 us (0.921)
  Pallas kernels: 50.2 us -> 46.6 us
  local copies, waits for them, and re-layouts: 3.03 us -> 1.66 us
  other arithmetic: 0 us -> 0.71 us
    pallas_call x1, Pallas kernels: 50.2 us -> 46.6 us  [local(): pl.pallas_call(functools.partial(kernel, L, R, Z, nc), out_shape=jax.Shap...]
    unnamed x7 -> x3, local copies, waits for them, and re-layouts: 3.03 us -> 1.66 us
    another operation x0 -> x1, other arithmetic: none -> 0.71 us  [local(): jnp.stack([density_mask.T, hamilton_mask.T, filter_mask.T])]
where the time goes in v4:
time: 49.2 us; the launch traced here: 49 us
  Pallas kernels  46.6 us (95%)
  local copies, waits for them, and re-layouts  1.66 us (3%)
  other arithmetic  0.71 us (1%)
    pallas_call x1, Pallas kernels, local(): pl.pallas_call(functools.partial(kernel, L, R, Z, nc), out_shape=jax.Shap...  46.6 us
    unnamed x3, local copies, waits for them, and re-layouts  1.66 us

profile of v4, /device:TPU:0, one launch (start us, length us, event | category | flops | bytes accessed | tf_op | source)
XLA Modules:
  0.0 49.0 jit_solution(840288800283456132)
XLA Ops:
  0.0 0.0 copy-start
  0.0 0.7 %copy-done = s32[16,8]{0,1:T(8,128)S(1)} copy-done((s32[16,8]{0,1:T(8,128)S(1)}, s32[16,8]{0,1:T(8,128)}, u32[]{:S(2)}) %copy-start) | copy-done | bytes 536
  0.7 0.7 %pad_add_fusion.m_in = s32[3,8,16]{2,1,0:T(8,128)S(1)} fusion(s32[1,8,16]{2,1,0:T(8,128)S(1)} %bitcast.9, s32[1,8,16]{2,1,0:T(8,128)} %bitcast.10, s32[1,8,16]{2,1,0:T(8,128)} %bitcast.11), kind=kLoop, calls=%fused_computation | loop fusion | flops 768 | bytes 3072 | tf_op jit(solution)/shard_map/stack | solution.py:386
  1.4 46.6 %shard_map.55 = bf16[1024,512]{1,0:T(8,128)(2,1)S(1)} custom-call(bf16[1024,512]{1,0:T(8,128)(2,1)} %p_hbm.1, bf16[1024,512]{1,0:T(8,128)(2,1)} %h_hbm.1, s32[3,8,16]{2,1,0:T(8,128)S(1)} %pad_add_fusion.m_in), custom_call_target="tpu_custom_call" | custom-call | flops 1073741824 | bytes 3145728 | tf_op jit(solution)/shard_map/pallas_call | solution.py:358
  48.0 1.0 %copy.7 = bf16[1024,512]{1,0:T(8,128)(2,1)} copy(bf16[1024,512]{1,0:T(8,128)(2,1)S(1)} %shard_map.55) | data formatting | bytes 2097152
Async XLA Ops:
  0.0 0.7 %copy-start = (s32[16,8]{0,1:T(8,128)S(1)}, s32[16,8]{0,1:T(8,128)}, u32[]{:S(2)}) copy-start(s32[16,8]{0,1:T(8,128)} %param.9) | copy-start | bytes 1540

commit v5 on v4

--- a/solution.py
+++ b/solution.py
@@ -153,9 +153,10 @@
             @pl.when(z_gets(ph, side, d))
             def _():
                 o = z_origin(side, d)
-                acc[rows, :] += jnp.dot(left[o, rows, :], right[o], preferred_element_type=F32)
-                if helped and ph == 1:
+                if right is pe and helped:
                     acc_e[...] += jnp.dot(left[o, rows, :], pe[o], preferred_element_type=F32)
+                else:
+                    acc[rows, :] += jnp.dot(left[o, rows, :], right[o], preferred_element_type=F32)
 
     def share(row, layer):
         start = layer * lr
@@ -184,8 +185,8 @@
 
     def end_copy(k):
         return pltpu.make_async_remote_copy(
-            we.at[pl.ds(k * cw, cw)],
-            out_ref.at[pl.ds(pl.multiple_of(l * lr + k * cw, cw), cw)],
+            we.at[pl.ds(k * ch, ch)],
+            out_ref.at[pl.ds(pl.multiple_of(l * lr + k * ch, ch), ch)],
             es.at[k], er.at[k], device_id={"col": beside})
 
     def w_copy(k, j, owner):
@@ -246,13 +247,13 @@
             for t in (1, 2):
                 turn_copy(2 * kw + (i + t + 1) % 2, t, l, t - 1).start()
         if kw > 0:
-            w_turns(kw - 1)
-
-    def w_turns(kw):
-        for k in (2 * kw, 2 * kw + 1):
-            t = via(k)
-            turn_copy(k, t, flip(t), t - 1).wait_recv()
-            turn_copy(k, 3 - t, flip(t), 2).start()
+            w_turn(2 * kw - 2)
+            w_turn(2 * kw - 1)
+
+    def w_turn(k):
+        t = via(k)
+        turn_copy(k, t, flip(t), t - 1).wait_recv()
+        turn_copy(k, 3 - t, flip(t), 2).start()
 
     def last_product(kw):
         rows = pl.ds(kw * cw, cw)
@@ -274,10 +275,16 @@
         for d in range(1, Z):
             for k in (2 * kw, 2 * kw + 1):
                 z_step(qg, 1, k, d)
-            add(1, qg, pc, rows, d)
+            if helped:
+                add(1, qg, pe, rows, d)
+            if not helped or d < Z - 2:
+                add(1, qg, pc, rows, d)
         if helped:
             we[rows, :] = acc_e[...].astype(BF)
-            end_copy(kw).start()
+            for k in (2 * kw, 2 * kw + 1):
+                end_copy(k).start()
+            add(1, qg, pc, rows, Z - 2)
+            add(1, qg, pc, rows, Z - 1)
         out_ref[pl.ds(pl.multiple_of(l * lr + kw * cw, cw), cw), :] = acc[rows, :].astype(BF)
         w_sends(kw)
 
@@ -289,16 +296,20 @@
 
         @pl.when(jnp.logical_not(middle))
         def _():
-            for kw in range(nw):
-                end_copy(kw).wait_recv()
-                w_sends(kw)
-
-        w_turns(nw - 1)
+            for k in range(nc):
+                end_copy(k).wait_recv()
+                for t in (via(k), 3 - via(k)):
+                    turn_copy(k, t, l, t - 1).start()
+                if 0 < k < nc - 1:
+                    w_turn(k - 1)
+
+        w_turn(nc - 2)
+        w_turn(nc - 1)
 
         @pl.when(middle)
         def _():
-            for kw in range(nw):
-                end_copy(kw).wait_send()
+            for k in range(nc):
+                end_copy(k).wait_send()
             for t in (1, 2):
                 share_copy(t, l).wait_send()
             for q in range(1, R):
@@ -350,8 +361,8 @@
             dma((2,)),
             dma((R - 1, L)),
             dma((R - 1, L)),
-            dma((nc // 2,)),
-            dma((nc // 2,)),
+            dma((nc,)),
+            dma((nc,)),
             dma((1,)),
             dma((1,)),
         ] if Z == 4 and L == 4 else []

time: 49.2 us -> 48.9 us (level)
  no operation moved by 1% of the time
where the time goes in v5:
time: 48.9 us; the launch traced here: 48.7 us
  Pallas kernels  46.3 us (95%)
  local copies, waits for them, and re-layouts  1.66 us (3%)
  other arithmetic  0.71 us (1%)
    pallas_call x1, Pallas kernels, local(): pl.pallas_call(functools.partial(kernel, L, R, Z, nc), out_shape=jax.Shap...  46.3 us
    unnamed x3, local copies, waits for them, and re-layouts  1.66 us

profile of v5, /device:TPU:0, one launch (start us, length us, event | category | flops | bytes accessed | tf_op | source)
XLA Modules:
  0.0 48.7 jit_solution(4246260613924604635)
XLA Ops:
  0.0 0.0 copy-start
  0.0 0.7 %copy-done = s32[16,8]{0,1:T(8,128)S(1)} copy-done((s32[16,8]{0,1:T(8,128)S(1)}, s32[16,8]{0,1:T(8,128)}, u32[]{:S(2)}) %copy-start) | copy-done | bytes 536
  0.7 0.7 %pad_add_fusion.m_in = s32[3,8,16]{2,1,0:T(8,128)S(1)} fusion(s32[1,8,16]{2,1,0:T(8,128)S(1)} %bitcast.9, s32[1,8,16]{2,1,0:T(8,128)} %bitcast.10, s32[1,8,16]{2,1,0:T(8,128)} %bitcast.11), kind=kLoop, calls=%fused_computation | loop fusion | flops 768 | bytes 3072 | tf_op jit(solution)/shard_map/stack | solution.py:397
  1.4 46.3 %shard_map.55 = bf16[1024,512]{1,0:T(8,128)(2,1)S(1)} custom-call(bf16[1024,512]{1,0:T(8,128)(2,1)} %p_hbm.1, bf16[1024,512]{1,0:T(8,128)(2,1)} %h_hbm.1, s32[3,8,16]{2,1,0:T(8,128)S(1)} %pad_add_fusion.m_in), custom_call_target="tpu_custom_call" | custom-call | flops 1073741824 | bytes 3145728 | tf_op jit(solution)/shard_map/pallas_call | solution.py:369
  47.7 1.0 %copy.7 = bf16[1024,512]{1,0:T(8,128)(2,1)} copy(bf16[1024,512]{1,0:T(8,128)(2,1)S(1)} %shard_map.55) | data formatting | bytes 2097152
Async XLA Ops:
  0.0 0.7 %copy-start = (s32[16,8]{0,1:T(8,128)S(1)}, s32[16,8]{0,1:T(8,128)}, u32[]{:S(2)}) copy-start(s32[16,8]{0,1:T(8,128)} %param.9) | copy-start | bytes 1540

commit v6 on v5

--- a/solution.py
+++ b/solution.py
@@ -118,7 +118,8 @@
         mask_chunk(k)
         if k == 0:
             pl.semaphore_wait(barrier, near + (R - 1) + (L - 1))
-        z_send(pg, 0, k, 0)
+        if k < 2:
+            z_send(pg, 0, k, 0)
 
     def fill(src, dst, e):
         per = tc // BS
@@ -195,36 +196,39 @@
             view, view, ws.at[j - 1, k], wr.at[j - 1, k],
             device_id={"layer": lax.rem(l + j, L)})
 
-    everything = pl.ds(0, lr)
-    for d in range(1, Z - 1):
-        for k in range(nc):
-            z_step(pg, 0, k, d)
-        if d == 1:
-            for j in range(1, R):
-                row_copy(hg, hs, hr, j, lax.rem(r + R - j, R)).wait_recv()
-            begin(pg, hg, everything)
-            if helped:
-                @pl.when(jnp.logical_not(middle))
-                def _():
-                    far_copy().start()
-
-                @pl.when(middle)
-                def _():
-                    share(r, l)[...] = pg[end]
-                    for t in (1, 2):
-                        share_copy(t, l).start()
-                    for q in range(1, R):
-                        pass_copy(q, 0, r, l).start()
-        add(0, pg, hg, everything, d)
-    for k in range(nc):
-        z_step(pg, 0, k, Z - 1)
-        add(0, pg, hg, pl.ds(k * ch, ch), Z - 1)
-        for i in range(ch // BS):
-            at = k * (ch // BS) + i
-            rows = pl.ds(at * BS, BS)
-            keep = em[2, pl.ds(l * lb + at, 1), :].astype(BF)
-            qg[c, rows, :] = acc[rows, :].astype(BF) * keep
-        z_send(qg, 1, k, 0)
+    for kw in range(nw):
+        pair = pl.ds(kw * cw, cw)
+        for d in range(1, Z):
+            for k in (2 * kw, 2 * kw + 1):
+                z_step(pg, 0, k, d)
+            if d == 1:
+                for k in (2 * kw + 2, 2 * kw + 3):
+                    if k < nc:
+                        z_send(pg, 0, k, 0)
+                if kw == 0:
+                    for j in range(1, R):
+                        row_copy(hg, hs, hr, j, lax.rem(r + R - j, R)).wait_recv()
+                if kw == nw - 1 and helped:
+                    @pl.when(jnp.logical_not(middle))
+                    def _():
+                        far_copy().start()
+
+                    @pl.when(middle)
+                    def _():
+                        share(r, l)[...] = pg[end]
+                        for t in (1, 2):
+                            share_copy(t, l).start()
+                        for q in range(1, R):
+                            pass_copy(q, 0, r, l).start()
+                begin(pg, hg, pair)
+            add(0, pg, hg, pair, d)
+        for k in (2 * kw, 2 * kw + 1):
+            for i in range(ch // BS):
+                at = k * (ch // BS) + i
+                rows = pl.ds(at * BS, BS)
+                keep = em[2, pl.ds(l * lb + at, 1), :].astype(BF)
+                qg[c, rows, :] = acc[rows, :].astype(BF) * keep
+            z_send(qg, 1, k, 0)
 
     for j in range(1, R):
         row_copy(pc, cs, cr_sem, j, lax.rem(r + R - j, R)).wait_recv()

time: 48.9 us -> 55.6 us (1.14)
  Pallas kernels: 46.3 us -> 52.9 us
    pallas_call x1, Pallas kernels: 46.3 us -> 52.9 us  [local(): pl.pallas_call(functools.partial(kernel, L, R, Z, nc), out_shape=jax.Shap...]
where the time goes in v6:
time: 55.6 us; the launch traced here: 55.3 us
  Pallas kernels  52.9 us (95%)
  local copies, waits for them, and re-layouts  1.66 us (3%)
  other arithmetic  0.71 us (1%)
    pallas_call x1, Pallas kernels, local(): pl.pallas_call(functools.partial(kernel, L, R, Z, nc), out_shape=jax.Shap...  52.9 us
    unnamed x3, local copies, waits for them, and re-layouts  1.66 us

profile of v6, /device:TPU:0, one launch (start us, length us, event | category | flops | bytes accessed | tf_op | source)
XLA Modules:
  0.0 55.3 jit_solution(3091832489483404722)
XLA Ops:
  0.0 0.0 copy-start
  0.0 0.7 %copy-done = s32[16,8]{0,1:T(8,128)S(1)} copy-done((s32[16,8]{0,1:T(8,128)S(1)}, s32[16,8]{0,1:T(8,128)}, u32[]{:S(2)}) %copy-start) | copy-done | bytes 536
  0.7 0.7 %pad_add_fusion.m_in = s32[3,8,16]{2,1,0:T(8,128)S(1)} fusion(s32[1,8,16]{2,1,0:T(8,128)S(1)} %bitcast.9, s32[1,8,16]{2,1,0:T(8,128)} %bitcast.10, s32[1,8,16]{2,1,0:T(8,128)} %bitcast.11), kind=kLoop, calls=%fused_computation | loop fusion | flops 768 | bytes 3072 | tf_op jit(solution)/shard_map/stack | solution.py:401
  1.4 52.9 %shard_map.55 = bf16[1024,512]{1,0:T(8,128)(2,1)S(1)} custom-call(bf16[1024,512]{1,0:T(8,128)(2,1)} %p_hbm.1, bf16[1024,512]{1,0:T(8,128)(2,1)} %h_hbm.1, s32[3,8,16]{2,1,0:T(8,128)S(1)} %pad_add_fusion.m_in), custom_call_target="tpu_custom_call" | custom-call | flops 1073741824 | bytes 3145728 | tf_op jit(solution)/shard_map/pallas_call | solution.py:373
  54.4 1.0 %copy.7 = bf16[1024,512]{1,0:T(8,128)(2,1)} copy(bf16[1024,512]{1,0:T(8,128)(2,1)S(1)} %shard_map.55) | data formatting | bytes 2097152
Async XLA Ops:
  0.0 0.7 %copy-start = (s32[16,8]{0,1:T(8,128)S(1)}, s32[16,8]{0,1:T(8,128)}, u32[]{:S(2)}) copy-start(s32[16,8]{0,1:T(8,128)} %param.9) | copy-start | bytes 1540
